TPU v7x, 256 devices: a whole 4x4x8 slice. The times are simulated.
256 devices in a mesh: outer: 8 (over z), inner: 32 (over x, y, core).
Axes of the slice: x: 4, y: 4, z: 8, core: 2. Of those that a mesh axis runs over, the one named last changes fastest.
Arguments:
- b_leaf: float32 [65536, 64], P(('outer', 'inner')), may hold values from -6 to 6
- b_sep: float32 [2048, 64], P(('outer', 'inner')), may hold values from -6 to 6
- b_root: float32 [2048, 64], P(('outer', 'inner')), may hold values from -6 to 6
- leaf_linv: float32 [65536, 256], P(('outer', 'inner')), as said below
- leaf_uinv: float32 [65536, 256], P(('outer', 'inner')), as said below
- leaf_lower: float32 [65536, 256], P(('outer', 'inner')), as said below
- leaf_upper: float32 [65536, 256], P(('outer', 'inner')), as said below
- sep_rows: int32 [256, 256], P(('outer', 'inner')), may hold values from 0 to 255, as said below
- sep_linv: float32 [2048, 256], P(('outer', 'inner')), as said below
- sep_uinv: float32 [2048, 256], P(('outer', 'inner')), as said below
- sep_lower: float32 [2048, 2048], P(None, ('outer', 'inner')), as said below
- sep_upper: float32 [2048, 2048], P(('outer', 'inner')), as said below
- root_linv: float32 [2048, 2048], P(('outer', 'inner')), as said below
- root_uinv: float32 [2048, 2048], P(('outer', 'inner')), as said below
- basis_leaf: float32 [65536, 512], P(('outer', 'inner')), as said below
- basis_sep: float32 [2048, 512], P(('outer', 'inner')), as said below
- basis_root: float32 [2048, 512], P(('outer', 'inner')), as said below
- g_blocks: float32 [262144, 128], P(('outer', 'inner')), may hold values from -0.25 to 0.25
- c_blocks: float32 [262144, 128], P(('outer', 'inner')), may hold values from -0.25 to 0.25
- block_cols: int32 [512, 4], P(('outer', 'inner')), may hold values from 0 to 1
Outputs:
- v_leaf: float32 [65536, 64], P(('outer', 'inner'))
- v_sep: float32 [2048, 64], P(('outer', 'inner'))
- v_root: float32 [2048, 64], P(('outer', 'inner'))
- coefficients: float32 [512, 64], replicated
- reduced_g: float32 [64, 64], replicated
- reduced_c: float32 [64, 64], replicated
Inputs may be any that keep to these rules, and one draw needn't show every extreme that they name: `sep_rows`: each row holds 256 distinct numbers; every row names 0 and 255. `leaf_linv`: lower triangular in each diagonal block of the stack, nonzero diagonal. `leaf_uinv`: upper triangular in each diagonal block of the stack, nonzero diagonal. `sep_linv`: lower triangular in each block of 256 rows, nonzero diagonal. `sep_uinv`: upper triangular in each block of 256 rows, nonzero diagonal. `root_linv`: lower triangular, nonzero diagonal. `root_uinv`: upper triangular, nonzero diagonal. `leaf_lower`: entries of order one over the square root of 256. `leaf_upper`: entries of order one over the square root of 256. `sep_lower`: entries of order one over the square root of the number of its columns. `sep_upper`: entries of order one over the square root of 2048. basis_leaf, basis_sep and basis_root stacked by rows form Q with Q^T Q = 69632 I up to float32 rounding. `basis_sep`: part of the stacked Q described with basis_leaf. `basis_root`: part of the stacked Q described with basis_leaf.
All inputs are finite; a program needn't handle non-finite values.
Results may differ from a plain program's by a relative error of at most 0.0003.
Values sent between devices are 32-bit elements; how exact they have to be, the bound alone decides.
A program may use at most 64 MiB of HBM per device.

v0:
```python
import jax
import jax.numpy as jnp
from jax import lax
from jax.sharding import PartitionSpec as P


def matmul_exact(left, right):
    return jnp.dot(left, right, precision=lax.Precision.HIGHEST, preferred_element_type=jnp.float32)


def contract_rows(left, right):
    return lax.dot_general(
        left,
        right,
        (((0,), (0,)), ((), ())),
        precision=lax.Precision.HIGHEST,
        preferred_element_type=jnp.float32,
    )


def shards(
    b_leaf,
    b_sep,
    b_root,
    leaf_linv,
    leaf_uinv,
    leaf_lower,
    leaf_upper,
    sep_rows,
    sep_linv,
    sep_uinv,
    sep_lower,
    sep_upper,
    root_linv,
    root_uinv,
    basis_leaf,
    basis_sep,
    basis_root,
    g_blocks,
    c_blocks,
    block_cols,
):
    ports = b_leaf.shape[1]
    sep_local = b_sep.shape[0]
    root_local = b_root.shape[0]
    sep_width = sep_linv.shape[1]
    selector = (sep_rows[0][:, None] == jnp.arange(sep_width, dtype=jnp.int32)[None, :]).astype(
        jnp.float32
    )
    y_leaf = matmul_exact(leaf_linv, b_leaf)
    contrib = matmul_exact(leaf_lower, y_leaf)
    t_sep = lax.psum_scatter(
        contract_rows(selector, contrib), "inner", scatter_dimension=0, tiled=True
    )
    sep_whole = lax.all_gather(b_sep - t_sep, "inner", axis=0, tiled=True)
    y_sep = matmul_exact(sep_linv, sep_whole)
    t_root = lax.psum_scatter(
        matmul_exact(sep_lower, y_sep), ("outer", "inner"), scatter_dimension=0, tiled=True
    )
    root_rhs = lax.all_gather(b_root - t_root, ("outer", "inner"), axis=0, tiled=True)
    y_root = matmul_exact(root_linv, root_rhs)
    y_root_all = lax.all_gather(y_root, ("outer", "inner"), axis=0, tiled=True)
    x_root = matmul_exact(root_uinv, y_root_all)
    x_root_all = lax.all_gather(x_root, ("outer", "inner"), axis=0, tiled=True)
    z_sep = y_sep - matmul_exact(sep_upper, x_root_all)
    z_sep_all = lax.all_gather(z_sep, "inner", axis=0, tiled=True)
    x_sep = matmul_exact(sep_uinv, z_sep_all)
    x_sep_all = lax.all_gather(x_sep, "inner", axis=0, tiled=True)
    coupled = matmul_exact(selector, x_sep_all)
    x_leaf = matmul_exact(leaf_uinv, y_leaf - matmul_exact(leaf_upper, coupled))
    node_count = float(
        lax.axis_size("outer") * lax.axis_size("inner") * (b_leaf.shape[0] + sep_local + root_local)
    )
    pieces_x = (x_leaf, x_sep, x_root)
    pieces_q = (basis_leaf, basis_sep, basis_root)
    projected = (
        contract_rows(basis_leaf, x_leaf)
        + contract_rows(basis_sep, x_sep)
        + contract_rows(basis_root, x_root)
    )
    coefficients = lax.psum(projected, ("outer", "inner")) / node_count
    cleaned = [
        values - matmul_exact(basis, coefficients) for basis, values in zip(pieces_q, pieces_x)
    ]
    local_gram = (
        contract_rows(cleaned[0], cleaned[0])
        + contract_rows(cleaned[1], cleaned[1])
        + contract_rows(cleaned[2], cleaned[2])
    )
    gram_matrix = lax.psum(local_gram, ("outer", "inner")) / node_count
    chol_lower = jnp.linalg.cholesky(gram_matrix)
    inverse_lower = lax.linalg.triangular_solve(
        chol_lower, jnp.eye(ports, dtype=jnp.float32), left_side=True, lower=True
    )
    v_leaf = matmul_exact(cleaned[0], inverse_lower.T)
    v_sep = matmul_exact(cleaned[1], inverse_lower.T)
    v_root = matmul_exact(cleaned[2], inverse_lower.T)
    block_rows = block_cols.shape[0]
    stored = block_cols.shape[1]
    block_size = g_blocks.shape[1]
    blocked = v_leaf.reshape(block_rows, block_size, ports)
    picked = blocked[block_cols]
    g_tiles = g_blocks.reshape(block_rows, stored, block_size, block_size)
    c_tiles = c_blocks.reshape(block_rows, stored, block_size, block_size)
    g_image = jnp.einsum("rwij,rwjp->rip", g_tiles, picked, precision=lax.Precision.HIGHEST)
    c_image = jnp.einsum("rwij,rwjp->rip", c_tiles, picked, precision=lax.Precision.HIGHEST)
    g_local = jnp.einsum("rip,riq->pq", blocked, g_image, precision=lax.Precision.HIGHEST)
    c_local = jnp.einsum("rip,riq->pq", blocked, c_image, precision=lax.Precision.HIGHEST)
    g_summed, c_summed = lax.psum((g_local, c_local), ("outer", "inner"))
    return (v_leaf, v_sep, v_root, coefficients, g_summed / node_count, c_summed / node_count)


def solution(mesh):
    return jax.shard_map(
        shards,
        mesh=mesh,
        in_specs=(
            P(("outer", "inner"), None),
            P(("outer", "inner"), None),
            P(("outer", "inner"), None),
            P(("outer", "inner"), None),
            P(("outer", "inner"), None),
            P(("outer", "inner"), None),
            P(("outer", "inner"), None),
            P(("outer", "inner"), None),
            P(("outer", "inner"), None),
            P(("outer", "inner"), None),
            P(None, ("outer", "inner")),
            P(("outer", "inner"), None),
            P(("outer", "inner"), None),
            P(("outer", "inner"), None),
            P(("outer", "inner"), None),
            P(("outer", "inner"), None),
            P(("outer", "inner"), None),
            P(("outer", "inner"), None),
            P(("outer", "inner"), None),
            P(("outer", "inner"), None),
        ),
        out_specs=(
            P(("outer", "inner"), None),
            P(("outer", "inner"), None),
            P(("outer", "inner"), None),
            P(),
            P(),
            P(),
        ),
        check_vma=False,
    )
```

profile of v0, /device:TPU:1, one launch (start us, length us, event | category | flops | bytes accessed | tf_op | source)
XLA Modules:
  0.0 1057.3 jit_solution(8577901284034292284)
XLA Ops:
  7.2 1.4 fusion.16
  9.7 1.0 fusion.8
  12.7 112.8 %all-reduce.9.cloned.1.call-done = f32[256,64]{1,0:T(8,128)} async-done(((f32[256,64]{1,0:T(8,128)}), f32[256,64]{1,0:T(8,128)}) %all-reduce.9.cloned.1.call-update) | async-done | bytes 65552
  125.5 0.7 dynamic-slice_subtract_fusion.1
  126.2 25.7 %all_gather.18 = f32[256,64]{1,0:T(8,128)S(1)} all-gather(f32[8,64]{1,0:T(8,128)S(1)} %dynamic-slice_subtract_fusion.1), channel_id=1, replica_groups=mesh['outer'=8,'inner'=32] {'inner'}, dimensions={0}, use_global_device_ids=true | all-gather | bytes 67584 | tf_op jit(solution)/shard_map/all_gather | solution.py:55
  153.3 1.3 copy.47
  155.4 251.8 %all-reduce.11.cloned.1.call-done = f32[2048,64]{1,0:T(8,128)} async-done(((f32[2048,64]{1,0:T(8,128)}), f32[2048,64]{1,0:T(8,128)}) %all-reduce.11.cloned.1.call-update) | async-done | bytes 524304
  407.2 0.7 dynamic-slice_subtract_fusion
  407.9 63.2 %all_gather.19 = f32[2048,64]{1,0:T(8,128)S(1)} all-gather(f32[8,64]{1,0:T(8,128)S(1)} %dynamic-slice_subtract_fusion), channel_id=1, replica_groups=mesh['outer'=8,'inner'=32] {'outer','inner'}, dimensions={0}, use_global_device_ids=true | all-gather | bytes 526336 | tf_op jit(solution)/shard_map/all_gather | solution.py:60
  471.7 60.2 %all_gather.20 = f32[2048,64]{1,0:T(8,128)S(1)} all-gather(f32[8,64]{1,0:T(8,128)S(1)} %convolution_bitcast_fusion.8), channel_id=1, replica_groups=mesh['outer'=8,'inner'=32] {'outer','inner'}, dimensions={0}, use_global_device_ids=true | all-gather | bytes 526336 | tf_op jit(solution)/shard_map/all_gather | solution.py:62
  532.6 60.4 %all_gather.21 = f32[2048,64]{1,0:T(8,128)S(1)} all-gather(f32[8,64]{1,0:T(8,128)S(1)} %bitcast.121), channel_id=1, replica_groups=mesh['outer'=8,'inner'=32] {'outer','inner'}, dimensions={0}, use_global_device_ids=true | all-gather | bytes 526336 | tf_op jit(solution)/shard_map/all_gather | solution.py:64
  593.7 23.3 %all_gather.22 = f32[256,64]{1,0:T(8,128)S(1)} all-gather(f32[8,64]{1,0:T(8,128)S(1)} %fusion.5), channel_id=1, replica_groups=mesh['outer'=8,'inner'=32] {'inner'}, dimensions={0}, use_global_device_ids=true | all-gather | bytes 67584 | tf_op jit(solution)/shard_map/all_gather | solution.py:66
  617.2 23.0 %all_gather.23 = f32[256,64]{1,0:T(8,128)S(1)} all-gather(f32[8,64]{1,0:T(8,128)S(1)} %bitcast.122), channel_id=1, replica_groups=mesh['outer'=8,'inner'=32] {'inner'}, dimensions={0}, use_global_device_ids=true | all-gather | bytes 67584 | tf_op jit(solution)/shard_map/all_gather | solution.py:68
  642.0 1.1 fusion.1
  643.1 237.7 %all-reduce.7.cloned.1.call-done = f32[512,64]{0,1:T(8,128)} async-done(((f32[512,64]{0,1:T(8,128)}), f32[512,64]{0,1:T(8,128)}) %all-reduce.7.cloned.1.call-update) | async-done | bytes 131088 | tf_op jit(solution)/shard_map/psum | solution.py:81
  880.8 0.9 broadcast_multiply_fusion
  883.5 76.0 %psum.29 = f32[64,64]{0,1:T(8,128)S(1)} all-reduce(f32[64,64]{0,1:T(8,128)S(1)} %convolution_add_fusion.1), channel_id=1, replica_groups=mesh['outer'=8,'inner'=32] {'outer','inner'}, use_global_device_ids=true, to_apply=%region_3.0 | all-reduce | flops 4096 | bytes 32768 | tf_op jit(solution)/shard_map/psum | solution.py:90
  959.7 5.8 cholesky.17
  966.9 4.9 custom-call.6
  972.2 0.8 fusion.27
  973.0 0.8 fusion.26
  976.2 73.1 %all-reduce.2 = (f32[64,64]{0,1:T(8,128)S(1)}, f32[64,64]{0,1:T(8,128)S(1)}) all-reduce(f32[64,64]{0,1:T(8,128)S(1)} %convolution_bitcast_fusion.5, f32[64,64]{0,1:T(8,128)S(1)} %convolution_bitcast_fusion.4), channel_id=1, replica_groups=mesh['outer'=8,'inner'=32] {'outer','inner'}, use_global_device_ids=true, to_apply=%region_6.7 | all-reduce | flops 8192 | bytes 65536 | tf_op jit(solution)/shard_map/psum | solution.py:109
  1049.4 0.7 copy.57
  1050.1 0.7 copy.58
  (85 shorter events, 14.6 us)
Async XLA Ops:
  7.2 967.2 %copy-start = (f32[1024,128]{1,0:T(8,128)S(1)}, f32[1024,128]{1,0:T(8,128)}, u32[]{:S(2)}) copy-start(f32[1024,128]{1,0:T(8,128)} %param.38) | copy-start | bytes 1572868
  7.2 1.5 copy-start.6
  7.2 118.3 %all-reduce.9.cloned.1.call-start = ((), (), s32[]{:S(2)}) async-start(), calls=%async_computation.1 | async-start | bytes 262144
  9.0 0.7 copy-start.16
  10.8 396.5 %all-reduce.11.cloned.1.call-start = ((), (), s32[]{:S(2)}) async-start(), calls=%async_computation.2 | async-start | bytes 2097152
  10.8 0.7 copy-start.20
  11.5 114.0 %copy-start.17 = (f32[8,64]{1,0:T(8,128)S(1)}, f32[8,64]{1,0:T(8,128)}, u32[]{:S(2)}) copy-start(f32[8,64]{1,0:T(8,128)} %param.21) | copy-start | bytes 6148
  126.2 25.7 %copy-start.14 = (f32[8,256]{1,0:T(8,128)S(1)}, f32[8,256]{1,0:T(8,128)}, u32[]{:S(2)}) copy-start(f32[8,256]{1,0:T(8,128)} %param.28) | copy-start | bytes 24580
  151.8 0.8 copy-start.8
  154.7 0.7 copy-start.19
  154.7 252.5 %copy-start.18 = (f32[8,64]{1,0:T(8,128)S(1)}, f32[8,64]{1,0:T(8,128)}, u32[]{:S(2)}) copy-start(f32[8,64]{1,0:T(8,128)} %param.22) | copy-start | bytes 6148
  154.7 726.1 %all-reduce.7.cloned.1.call-start = ((), (), s32[]{:S(2)}) async-start(), calls=%async_computation | async-start | bytes 262144 | tf_op jit(solution)/shard_map/psum | solution.py:81
  407.9 63.2 %copy-start.9 = (f32[8,2048]{1,0:T(8,128)S(1)}, f32[8,2048]{1,0:T(8,128)}, u32[]{:S(2)}) copy-start(f32[8,2048]{1,0:T(8,128)} %param.32) | copy-start | bytes 196612
  471.7 60.2 %copy-start.10 = (f32[8,2048]{1,0:T(8,128)S(1)}, f32[8,2048]{1,0:T(8,128)}, u32[]{:S(2)}) copy-start(f32[8,2048]{1,0:T(8,128)} %param.33) | copy-start | bytes 196612
  532.6 60.4 %copy-start.11 = (f32[8,2048]{1,0:T(8,128)S(1)}, f32[8,2048]{1,0:T(8,128)}, u32[]{:S(2)}) copy-start(f32[8,2048]{1,0:T(8,128)} %param.31) | copy-start | bytes 196612
  593.7 23.3 %copy-start.15 = (f32[8,256]{1,0:T(8,128)S(1)}, f32[8,256]{1,0:T(8,128)}, u32[]{:S(2)}) copy-start(f32[8,256]{1,0:T(8,128)} %param.29) | copy-start | bytes 24580
  617.2 23.4 %copy-start.12 = (f32[8,512]{1,0:T(8,128)S(1)}, f32[8,512]{1,0:T(8,128)}, u32[]{:S(2)}) copy-start(f32[8,512]{1,0:T(8,128)} %param.35) | copy-start | bytes 49156
  640.2 0.7 copy-start.13
  640.2 1.0 copy-start.5
  640.6 1.1 copy-start.7
  640.9 1.1 copy-start.1
  881.8 0.8 copy-start.2
  972.2 3.8 copy-start.3
  974.3 1.0 copy-start.4
Sparse Core Ops, SparseCore 0:
  11.8 113.6 all-reduce.8
  154.8 252.3 all-reduce.10
  643.3 237.5 all-reduce.6
where the time goes:
time: 1060 us
  waiting for transfers between devices  602 us (57%)
  blocking collectives  405 us (38%)
  between operations  14.7 us (1%)
  other arithmetic  14.4 us (1%)
  matrix products  14 us (1%)
    unnamed x5, waiting for transfers between devices  365 us
    psum x1, waiting for transfers between devices, shards(): coefficients = lax.psum(projected, ('outer', 'inner')) / node_count  238 us
    psum x1, blocking collectives, shards(): gram_matrix = lax.psum(local_gram, ('outer', 'inner')) / node_count  76 us
    psum x1, blocking collectives, shards(): g_summed, c_summed = lax.psum((g_local, c_local), ('outer', 'inner'))  73.1 us
    all_gather x1, blocking collectives, shards(): lax.all_gather(b_root - t_root, ('outer', 'inner'), axis=0, tiled=True)  63.2 us
    all_gather x1, blocking collectives, shards(): x_root_all = lax.all_gather(x_root, ('outer', 'inner'), axis=0, tiled=True)  60.4 us
    all_gather x1, blocking collectives, shards(): y_root_all = lax.all_gather(y_root, ('outer', 'inner'), axis=0, tiled=True)  60.2 us
    all_gather x1, blocking collectives, shards(): sep_whole = lax.all_gather(b_sep - t_sep, 'inner', axis=0, tiled=True)  25.7 us
  transfers between devices with their start and end apart: 3, of which 3 were waited for; matrix products, arithmetic and copies ran while one was open for 0% of the time, Pallas kernels for 0%

commit v1 on v0

--- a/solution.py
+++ b/solution.py
@@ -2,6 +2,12 @@
 import jax.numpy as jnp
 from jax import lax
 from jax.sharding import PartitionSpec as P
+
+
+def divide_blocks(inp, named_axis, across):
+    for it in (named_axis, across):
+        inp = jax.lax.psum(inp, axis_name=it)
+    return inp
 
 
 def matmul_exact(left, right):
@@ -78,7 +84,7 @@
         + contract_rows(basis_sep, x_sep)
         + contract_rows(basis_root, x_root)
     )
-    coefficients = lax.psum(projected, ("outer", "inner")) / node_count
+    coefficients = divide_blocks(projected, "outer", "inner") / node_count
     cleaned = [
         values - matmul_exact(basis, coefficients) for basis, values in zip(pieces_q, pieces_x)
     ]

time: 1060 us -> 1000 us (0.943)
  waiting for transfers between devices: 602 us -> 545 us
    psum x1 -> x2, waiting for transfers between devices: 238 us -> 180 us  [divide_blocks(): inp = jax.lax.psum(inp, axis_name=it)]
    unnamed x5 -> x6, waiting for transfers between devices: 365 us -> 365 us
  transfers between devices with their start and end apart: 3 -> 4, of which waited for: 3 -> 4; matrix products, arithmetic and copies ran while one was open for 0% -> 0% of each run, Pallas kernels for 0% -> 0%
where the time goes in v1:
time: 1000 us
  waiting for transfers between devices  545 us (54%)
  blocking collectives  407 us (41%)
  between operations  14.7 us (1%)
  other arithmetic  14.4 us (1%)
  matrix products  14 us (1%)
    unnamed x6, waiting for transfers between devices  365 us
    psum x2, waiting for transfers between devices, divide_blocks(): inp = jax.lax.psum(inp, axis_name=it)  180 us
    psum x1, blocking collectives, shards(): gram_matrix = lax.psum(local_gram, ('outer', 'inner')) / node_count  76.9 us
    psum x1, blocking collectives, shards(): g_summed, c_summed = lax.psum((g_local, c_local), ('outer', 'inner'))  74 us
    all_gather x1, blocking collectives, shards(): lax.all_gather(b_root - t_root, ('outer', 'inner'), axis=0, tiled=True)  63.2 us
    all_gather x1, blocking collectives, shards(): x_root_all = lax.all_gather(x_root, ('outer', 'inner'), axis=0, tiled=True)  60.4 us
    all_gather x1, blocking collectives, shards(): y_root_all = lax.all_gather(y_root, ('outer', 'inner'), axis=0, tiled=True)  60.2 us
    all_gather x1, blocking collectives, shards(): sep_whole = lax.all_gather(b_sep - t_sep, 'inner', axis=0, tiled=True)  25.7 us
  transfers between devices with their start and end apart: 4, of which 4 were waited for; matrix products, arithmetic and copies ran while one was open for 0% of the time, Pallas kernels for 0%

profile of v1, /device:TPU:1, one launch (start us, length us, event | category | flops | bytes accessed | tf_op | source)
XLA Modules:
  0.0 1001.8 jit_solution(6773892369940657298)
XLA Ops:
  7.2 1.4 fusion.16
  9.7 1.0 fusion.8
  12.7 112.8 %all-reduce.12.cloned.1.call-done = f32[256,64]{1,0:T(8,128)} async-done(((f32[256,64]{1,0:T(8,128)}), f32[256,64]{1,0:T(8,128)}) %all-reduce.12.cloned.1.call-update) | async-done | bytes 65552
  125.5 0.7 dynamic-slice_subtract_fusion.1
  126.2 25.7 %all_gather.18 = f32[256,64]{1,0:T(8,128)S(1)} all-gather(f32[8,64]{1,0:T(8,128)S(1)} %dynamic-slice_subtract_fusion.1), channel_id=1, replica_groups=mesh['outer'=8,'inner'=32] {'inner'}, dimensions={0}, use_global_device_ids=true | all-gather | bytes 67584 | tf_op jit(solution)/shard_map/all_gather | solution.py:61
  153.3 1.3 copy.47
  154.7 252.5 %all-reduce.14.cloned.1.call-done = f32[2048,64]{1,0:T(8,128)} async-done(((f32[2048,64]{1,0:T(8,128)}), f32[2048,64]{1,0:T(8,128)}) %all-reduce.14.cloned.1.call-update) | async-done | bytes 524304
  407.9 63.2 %all_gather.19 = f32[2048,64]{1,0:T(8,128)S(1)} all-gather(f32[8,64]{1,0:T(8,128)S(1)} %dynamic-slice_subtract_fusion), channel_id=1, replica_groups=mesh['outer'=8,'inner'=32] {'outer','inner'}, dimensions={0}, use_global_device_ids=true | all-gather | bytes 526336 | tf_op jit(solution)/shard_map/all_gather | solution.py:66
  471.7 60.2 %all_gather.20 = f32[2048,64]{1,0:T(8,128)S(1)} all-gather(f32[8,64]{1,0:T(8,128)S(1)} %convolution_bitcast_fusion.8), channel_id=1, replica_groups=mesh['outer'=8,'inner'=32] {'outer','inner'}, dimensions={0}, use_global_device_ids=true | all-gather | bytes 526336 | tf_op jit(solution)/shard_map/all_gather | solution.py:68
  532.6 60.4 %all_gather.21 = f32[2048,64]{1,0:T(8,128)S(1)} all-gather(f32[8,64]{1,0:T(8,128)S(1)} %bitcast.121), channel_id=1, replica_groups=mesh['outer'=8,'inner'=32] {'outer','inner'}, dimensions={0}, use_global_device_ids=true | all-gather | bytes 526336 | tf_op jit(solution)/shard_map/all_gather | solution.py:70
  593.7 23.3 %all_gather.22 = f32[256,64]{1,0:T(8,128)S(1)} all-gather(f32[8,64]{1,0:T(8,128)S(1)} %fusion.5), channel_id=1, replica_groups=mesh['outer'=8,'inner'=32] {'inner'}, dimensions={0}, use_global_device_ids=true | all-gather | bytes 67584 | tf_op jit(solution)/shard_map/all_gather | solution.py:72
  617.2 23.0 %all_gather.23 = f32[256,64]{1,0:T(8,128)S(1)} all-gather(f32[8,64]{1,0:T(8,128)S(1)} %bitcast.122), channel_id=1, replica_groups=mesh['outer'=8,'inner'=32] {'inner'}, dimensions={0}, use_global_device_ids=true | all-gather | bytes 67584 | tf_op jit(solution)/shard_map/all_gather | solution.py:74
  642.0 1.1 fusion.1
  643.9 63.0 %all-reduce.8.cloned.1.call-done = f32[512,64]{0,1:T(8,128)} async-done(((f32[512,64]{0,1:T(8,128)}), f32[512,64]{0,1:T(8,128)}) %all-reduce.8.cloned.1.call-update) | async-done | bytes 131088 | tf_op jit(solution)/shard_map/psum | solution.py:9
  706.9 116.7 %all-reduce.10.cloned.1.call-done = f32[512,64]{0,1:T(8,128)} async-done(((f32[512,64]{0,1:T(8,128)}), f32[512,64]{0,1:T(8,128)}) %all-reduce.10.cloned.1.call-update) | async-done | bytes 131088 | tf_op jit(solution)/shard_map/psum | solution.py:9
  823.6 0.9 broadcast_multiply_fusion
  826.3 76.9 %psum.37 = f32[64,64]{0,1:T(8,128)S(1)} all-reduce(f32[64,64]{0,1:T(8,128)S(1)} %convolution_add_fusion.1), channel_id=1, replica_groups=mesh['outer'=8,'inner'=32] {'outer','inner'}, use_global_device_ids=true, to_apply=%region_4.0 | all-reduce | flops 4096 | bytes 32768 | tf_op jit(solution)/shard_map/psum | solution.py:96
  903.3 5.8 cholesky.17
  910.5 4.9 custom-call.6
  915.8 0.8 fusion.27
  916.6 0.8 fusion.26
  919.9 74.0 %all-reduce.2 = (f32[64,64]{0,1:T(8,128)S(1)}, f32[64,64]{0,1:T(8,128)S(1)}) all-reduce(f32[64,64]{0,1:T(8,128)S(1)} %convolution_bitcast_fusion.5, f32[64,64]{0,1:T(8,128)S(1)} %convolution_bitcast_fusion.4), channel_id=1, replica_groups=mesh['outer'=8,'inner'=32] {'outer','inner'}, use_global_device_ids=true, to_apply=%region_7.8 | all-reduce | flops 8192 | bytes 65536 | tf_op jit(solution)/shard_map/psum | solution.py:115
  993.8 0.7 copy.57
  994.5 0.7 copy.58
  (88 shorter events, 15.3 us)
Async XLA Ops:
  7.2 910.8 %copy-start = (f32[1024,128]{1,0:T(8,128)S(1)}, f32[1024,128]{1,0:T(8,128)}, u32[]{:S(2)}) copy-start(f32[1024,128]{1,0:T(8,128)} %param.38) | copy-start | bytes 1572868
  7.2 1.5 copy-start.6
  7.2 118.3 %all-reduce.12.cloned.1.call-start = ((), (), s32[]{:S(2)}) async-start(), calls=%async_computation.2 | async-start | bytes 262144
  9.0 0.7 copy-start.16
  10.8 396.4 %all-reduce.14.cloned.1.call-start = ((), (), s32[]{:S(2)}) async-start(), calls=%async_computation.3 | async-start | bytes 2097152
  10.8 0.7 copy-start.20
  11.5 114.0 %copy-start.17 = (f32[8,64]{1,0:T(8,128)S(1)}, f32[8,64]{1,0:T(8,128)}, u32[]{:S(2)}) copy-start(f32[8,64]{1,0:T(8,128)} %param.21) | copy-start | bytes 6148
  126.2 25.7 %copy-start.14 = (f32[8,256]{1,0:T(8,128)S(1)}, f32[8,256]{1,0:T(8,128)}, u32[]{:S(2)}) copy-start(f32[8,256]{1,0:T(8,128)} %param.28) | copy-start | bytes 24580
  151.8 0.8 copy-start.8
  154.7 252.5 %copy-start.18 = (f32[8,64]{1,0:T(8,128)S(1)}, f32[8,64]{1,0:T(8,128)}, u32[]{:S(2)}) copy-start(f32[8,64]{1,0:T(8,128)} %param.22) | copy-start | bytes 6148
  154.7 552.2 %all-reduce.8.cloned.1.call-start = ((), (), s32[]{:S(2)}) async-start(), calls=%async_computation | async-start | bytes 262144 | tf_op jit(solution)/shard_map/psum | solution.py:9
  407.9 63.2 %copy-start.9 = (f32[8,2048]{1,0:T(8,128)S(1)}, f32[8,2048]{1,0:T(8,128)}, u32[]{:S(2)}) copy-start(f32[8,2048]{1,0:T(8,128)} %param.32) | copy-start | bytes 196612
  471.7 60.2 %copy-start.10 = (f32[8,2048]{1,0:T(8,128)S(1)}, f32[8,2048]{1,0:T(8,128)}, u32[]{:S(2)}) copy-start(f32[8,2048]{1,0:T(8,128)} %param.33) | copy-start | bytes 196612
  532.6 60.4 %copy-start.11 = (f32[8,2048]{1,0:T(8,128)S(1)}, f32[8,2048]{1,0:T(8,128)}, u32[]{:S(2)}) copy-start(f32[8,2048]{1,0:T(8,128)} %param.31) | copy-start | bytes 196612
  593.7 23.3 %copy-start.15 = (f32[8,256]{1,0:T(8,128)S(1)}, f32[8,256]{1,0:T(8,128)}, u32[]{:S(2)}) copy-start(f32[8,256]{1,0:T(8,128)} %param.29) | copy-start | bytes 24580
  617.2 23.4 %copy-start.12 = (f32[8,512]{1,0:T(8,128)S(1)}, f32[8,512]{1,0:T(8,128)}, u32[]{:S(2)}) copy-start(f32[8,512]{1,0:T(8,128)} %param.35) | copy-start | bytes 49156
  640.2 0.7 copy-start.13
  640.2 1.0 copy-start.5
  640.6 1.1 copy-start.7
  640.9 1.1 copy-start.1
  643.1 180.5 %all-reduce.10.cloned.1.call-start = ((), (), s32[]{:S(2)}) async-start(), calls=%async_computation.1 | async-start | bytes 262144 | tf_op jit(solution)/shard_map/psum | solution.py:9
  824.5 0.8 copy-start.2
  915.8 3.8 copy-start.3
  918.0 1.0 copy-start.4
  (1 other events, 0.7 us)
Sparse Core Ops, SparseCore 0:
  11.8 113.6 all-reduce.11
  154.8 252.3 all-reduce.13
  643.2 63.5 all-reduce.7
  710.3 113.2 all-reduce.9
